TPU v7x, 32 devices: a whole 2x2x4 slice. The times are simulated.
32 devices in a mesh: groups: 2 (over x), band: 16 (over z, y, core).
Axes of the slice: x: 2, y: 2, z: 4, core: 2. Of those that a mesh axis runs over, the one named last changes fastest.
Arguments:
- grid_latent: bfloat16 [24576, 512], P(('groups', 'band')), parts along dimension 0, may hold values from -6 to 6
- mesh_latent: bfloat16 [5120, 512], P(('groups', 'band')), parts along dimension 0, may hold values from -6 to 6
- grid_edges: bfloat16 [24576, 512], P('band'), may hold values from -6 to 6
- mesh_edges: bfloat16 [16384, 512], P('band'), may hold values from -6 to 6
- grid_slots: int32 [16, 16, 96], P('band'), may hold values from -1 to 767, as said below
- grid_senders: int32 [24576], P('band'), may hold values from 0 to 1535, as said below
- grid_receivers: int32 [24576], P('band'), may hold values from 0 to 160, as said below
- mesh_slots: int32 [16, 16, 32], P('band'), may hold values from -1 to 159, as said below
- mesh_senders: int32 [16384], P('band'), may hold values from 0 to 751, as said below
- mesh_receivers: int32 [16384], P('band'), may hold values from 0 to 160, as said below
- grid_node_in: bfloat16 [512, 512], replicated, may hold values from -0.25 to 0.25
- grid_node_out: bfloat16 [512, 512], replicated, may hold values from -0.25 to 0.25
- grid_node_vectors: float32 [2, 512], replicated, may hold values from -4 to 4
- encode_edge_in: bfloat16 [1536, 512], replicated, may hold values from -0.15625 to 0.15625
- encode_edge_out: bfloat16 [512, 512], replicated, may hold values from -0.25 to 0.25
- encode_edge_vectors: float32 [2, 512], replicated, may hold values from -4 to 4
- encode_node_in: bfloat16 [1024, 512], replicated, may hold values from -0.1875 to 0.1875
- encode_node_out: bfloat16 [512, 512], replicated, may hold values from -0.25 to 0.25
- encode_node_vectors: float32 [2, 512], replicated, may hold values from -4 to 4
- process_edge_in: bfloat16 [1536, 512], replicated, may hold values from -0.15625 to 0.15625
- process_edge_out: bfloat16 [512, 512], replicated, may hold values from -0.25 to 0.25
- process_edge_vectors: float32 [2, 512], replicated, may hold values from -4 to 4
- process_node_in: bfloat16 [1024, 512], replicated, may hold values from -0.1875 to 0.1875
- process_node_out: bfloat16 [512, 512], replicated, may hold values from -0.25 to 0.25
- process_node_vectors: float32 [2, 512], replicated, may hold values from -4 to 4
Outputs:
- grid_update: bfloat16 [24576, 512], P(('groups', 'band')), parts along dimension 0
- mesh_update: bfloat16 [5120, 512], P(('groups', 'band')), parts along dimension 0
There are 2 independent parts, one for each index of `groups`. A program takes and returns all parts, laid end to end along the dimension named above; an argument that names none is the same for every part. Nothing has to cross between parts.
Inputs may be any that keep to these rules, and one draw needn't show every extreme that they name: `grid_slots`: entry [s, d, k] is the row among device s's 768 grid rows that device s sends to device d in slot k, or -1 for an empty slot. In every pair the live slots come first and there is at least one; one destination gets all 96 slots from every source, and one source fills all 96 slots to every destination. `grid_senders`: each code is src * 96 + k where k is a live slot that device src sends to the edge's device; every device has edges reading from every source. `grid_receivers`: 160 marks a padding edge. Padding edges stand at the end of each device's 1536 rows, at least half of each device's rows are live, and some device has no padding. `mesh_slots`: entry [s, d, k] is the row among device s's 160 mesh rows that device s sends to device d in slot k, or -1 for an empty slot. In every pair the live slots come first and there is at least one; one destination gets all 32 slots from every source, and one source fills all 32 slots to every destination. `mesh_senders`: A code below 240 names one of the device's own rows or one of the 40 rows at the near end of a neighbouring device; the first device reads no row before its own, the last none after. A larger code is 240 + src * 32 + k with k a live slot that device src sends to the edge's device; every device has edges reading from every source. `mesh_receivers`: 160 marks a padding edge. Padding edges stand at the end of each device's 1024 rows, at least half of each device's rows are live, and some device has no padding.
All inputs are finite; a program needn't handle non-finite values.
Results may differ from a plain program's by a relative error of at most 0.008.
Values may be sent and summed in bfloat16 or wider, within the bound.
A program may use at most 64 MiB of HBM per device.

v0:
```python
import jax
import jax.numpy as jnp
from jax import lax
from jax.sharding import PartitionSpec as P


def extended(cells, sides, width):
    for axis, dim in sides:
        count = lax.axis_size(axis)
        ends = count - 1
        head = lax.slice_in_dim(cells, 0, width, axis=dim)
        tail = lax.slice_in_dim(cells, cells.shape[dim] - width, cells.shape[dim], axis=dim)
        cells = jnp.concatenate(
            [
                lax.ppermute(tail, axis, [(i, (i + 1) % count) for i in range(ends)]),
                cells,
                lax.ppermute(head, axis, [((i + 1) % count, i) for i in range(ends)]),
            ],
            axis=dim,
        )
    return cells


def product(left, right):
    return jnp.dot(left, right, preferred_element_type=jnp.float32)


def mlp_tail(preact, vectors, weight_out):
    hidden = jax.nn.silu(preact + vectors[0]).astype(jnp.bfloat16)
    output = product(hidden, weight_out)
    centred = output - jnp.mean(output, axis=-1, keepdims=True)
    spread = jnp.mean(centred * centred, axis=-1, keepdims=True)
    return centred * lax.rsqrt(spread + 1e-05) * vectors[1]


def edge_sums(
    sender_terms,
    sender_codes,
    edge_latent,
    receivers,
    receiver_terms,
    edge_weight,
    vectors,
    weight_out,
):
    mesh_count = receiver_terms.shape[0]
    preact = product(edge_latent, edge_weight)
    preact = preact + jnp.take(sender_terms, sender_codes, axis=0).astype(jnp.float32)
    preact = preact + jnp.take(receiver_terms, jnp.minimum(receivers, mesh_count - 1), axis=0)
    message = (edge_latent.astype(jnp.float32) + mlp_tail(preact, vectors, weight_out)).astype(
        jnp.bfloat16
    )
    blocks = edge_latent.shape[0] // 128
    targets = jnp.arange(mesh_count, dtype=jnp.int32).reshape(1, mesh_count, 1)
    onehot = (receivers.reshape(blocks, 1, 128) == targets).astype(jnp.bfloat16)
    return jnp.einsum(
        "bmk,bkl->ml",
        onehot,
        message.reshape(blocks, 128, message.shape[1]),
        preferred_element_type=jnp.float32,
    )


def pick_rows(table, slot_table):
    chosen = jnp.take(table, jnp.maximum(slot_table, 0), axis=0)
    return jnp.where((slot_table >= 0)[:, :, None], chosen, jnp.zeros((), table.dtype))


def local(
    grid_latent,
    mesh_latent,
    grid_edges,
    mesh_edges,
    grid_slots,
    grid_senders,
    grid_receivers,
    mesh_slots,
    mesh_senders,
    mesh_receivers,
    grid_node_in,
    grid_node_out,
    grid_node_vectors,
    encode_edge_in,
    encode_edge_out,
    encode_edge_vectors,
    encode_node_in,
    encode_node_out,
    encode_node_vectors,
    process_edge_in,
    process_edge_out,
    process_edge_vectors,
    process_node_in,
    process_node_out,
    process_node_vectors,
):
    latent_width = grid_latent.shape[1]
    sender_weight = encode_edge_in[latent_width : 2 * latent_width]
    own_terms = product(grid_latent, sender_weight).astype(jnp.bfloat16)
    arrived = lax.all_to_all(
        pick_rows(own_terms, grid_slots[0]), "band", split_axis=0, concat_axis=0, tiled=True
    )
    grid_terms = arrived.reshape(-1, latent_width)
    grid_branch = mlp_tail(product(grid_latent, grid_node_in), grid_node_vectors, grid_node_out)
    grid_update = (grid_latent.astype(jnp.float32) + grid_branch).astype(jnp.bfloat16)
    receiver_terms = product(mesh_latent, encode_edge_in[2 * latent_width :])
    encode_sum = edge_sums(
        grid_terms,
        grid_senders,
        grid_edges,
        grid_receivers,
        receiver_terms,
        encode_edge_in[:latent_width],
        encode_edge_vectors,
        encode_edge_out,
    )
    node_preact = product(mesh_latent, encode_node_in[:latent_width]) + product(
        encode_sum.astype(jnp.bfloat16), encode_node_in[latent_width:]
    )
    mesh_middle = (
        mesh_latent.astype(jnp.float32)
        + mlp_tail(node_preact, encode_node_vectors, encode_node_out)
    ).astype(jnp.bfloat16)
    rim_rows = mesh_middle.shape[0] // 4
    mesh_weight = process_edge_in[latent_width : 2 * latent_width]
    own_mesh = product(mesh_middle, mesh_weight).astype(jnp.bfloat16)
    near_terms = extended(own_mesh, (("band", 0),), rim_rows)
    far_terms = lax.all_to_all(
        pick_rows(own_mesh, mesh_slots[0]), "band", split_axis=0, concat_axis=0, tiled=True
    )
    mesh_terms = jnp.concatenate([near_terms, far_terms.reshape(-1, latent_width)], axis=0)
    middle_terms = product(mesh_middle, process_edge_in[2 * latent_width :])
    process_sum = edge_sums(
        mesh_terms,
        mesh_senders,
        mesh_edges,
        mesh_receivers,
        middle_terms,
        process_edge_in[:latent_width],
        process_edge_vectors,
        process_edge_out,
    )
    final_preact = product(mesh_middle, process_node_in[:latent_width]) + product(
        process_sum.astype(jnp.bfloat16), process_node_in[latent_width:]
    )
    mesh_update = (
        mesh_middle.astype(jnp.float32)
        + mlp_tail(final_preact, process_node_vectors, process_node_out)
    ).astype(jnp.bfloat16)
    return (grid_update, mesh_update)


def solution(mesh):
    return jax.shard_map(
        local,
        mesh=mesh,
        in_specs=(
            P(("groups", "band"), None),
            P(("groups", "band"), None),
            P("band", None),
            P("band", None),
            P("band", None, None),
            P("band"),
            P("band"),
            P("band", None, None),
            P("band"),
            P("band"),
            P(),
            P(),
            P(),
            P(),
            P(),
            P(),
            P(),
            P(),
            P(),
            P(),
            P(),
            P(),
            P(),
            P(),
            P(),
        ),
        out_specs=(P(("groups", "band"), None), P(("groups", "band"), None)),
        check_vma=False,
    )
```

profile of v0, /device:TPU:16, one launch (start us, length us, event | category | flops | bytes accessed | tf_op | source)
XLA Modules:
  0.0 113.2 jit_solution(166016199003778124)
XLA Ops:
  0.6 0.0 copy-start
  0.6 0.8 compare_bitcast_fusion.3
  1.4 0.7 broadcast_maximum_fusion.1
  2.1 0.1 reshape.166
  2.2 1.8 %convolution_convert_fusion = bf16[768,512]{1,0:T(8,128)(2,1)S(1)} fusion(bf16[768,512]{1,0:T(8,128)(2,1)} %param.25, bf16[1536,512]{1,0:T(8,128)(2,1)} %param.38), kind=kOutput, calls=%fused_computation.20 | convolution fusion | flops 403046400 | bytes 2097152 | tf_op jit(solution)/shard_map/dot_general | solution.py:25
  4.0 4.8 %gather_fusion = bf16[1536,512]{1,0:T(8,128)(2,1)S(1)} fusion(bf16[768,512]{1,0:T(8,128)(2,1)S(1)} %convolution_convert_fusion, s32[2048]{0:T(1024)S(1)} %pad_clamp_fusion.2), kind=kCustom, calls=%fused_computation | custom fusion | bytes 3151872 | tf_op jit(solution)/shard_map/jit(_take)/gather | solution.py:65
  8.9 1.5 %select_select_fusion = bf16[16,96,512]{2,1,0:T(8,128)(2,1)} fusion(bf16[16,96,512]{2,1,0:T(8,128)(2,1)S(1)} %bitcast.62, pred[16,96]{1,0:T(8,128)(4,1)S(1)} %get-tuple-element.9, pred[16,96]{1,0:T(8,128)(4,1)S(1)} %get-tuple-element.8), kind=kLoop, calls=%fused_computation.15 | loop fusion | flops 1572864 | bytes 3148800 | tf_op jit(solution)/shard_map/jit(_where)/select_n | solution.py:66
  10.3 6.3 %all-to-all-start = ((bf16[16,96,512]{2,1,0:T(8,128)(2,1)}), bf16[16,96,512]{2,1,0:T(8,128)(2,1)S(1)}, u32[]{:S(2)}, u32[]{:S(2)}) async-start(bf16[16,96,512]{2,1,0:T(8,128)(2,1)} %select_select_fusion), calls=%async_computation | async-start | bytes 3145728 | tf_op jit(solution)/shard_map/all_to_all | solution.py:99
  16.6 0.0 copy-done.7
  16.7 0.0 copy-start.11
  16.7 0.0 copy-start.5
  16.7 0.0 copy-start.12
  16.7 0.0 copy-start.10
  16.7 0.0 copy-start.15
  16.7 1.2 %copy.27 = bf16[768,512]{0,1:T(8,128)(2,1)} copy(bf16[768,512]{1,0:T(8,128)(2,1)S(1)} %copy-done.7) | data formatting | bytes 1572864 | tf_op args[0]
  17.9 0.0 copy-done.11
  17.9 0.0 copy-done.5
  17.9 1.3 %fusion.24 = f32[160,512]{1,0:T(8,128)S(1)} fusion(bf16[160,512]{1,0:T(8,128)(2,1)S(1)} %copy-done.5, bf16[1536,512]{1,0:T(8,128)(2,1)} %param.38), kind=kOutput, calls=%fused_computation.49 | convolution fusion | flops 83886080 | bytes 1015808 | tf_op jit(solution)/shard_map/dot_general | solution.py:25
  19.2 0.0 copy-done.12
  19.2 0.1 reshape.190
  19.3 4.9 %gather_fusion.2 = f32[1536,512]{1,0:T(8,128)} fusion(f32[160,512]{1,0:T(8,128)S(1)} %fusion.24, s32[2048]{0:T(1024)S(1)} %pad_clamp_fusion), kind=kCustom, calls=%fused_computation.2 | custom fusion | bytes 6297600 | tf_op jit(solution)/shard_map/jit(_take)/gather | solution.py:49
  24.3 0.0 copy-start.18
  24.3 3.7 %fusion.54 = (f32[768]{0:T(1024)S(1)}, f32[768,512]{0,1:T(8,128)}) fusion(bf16[512,512]{1,0:T(8,128)(2,1)} %param.36, bf16[768,512]{1,0:T(8,128)(2,1)} %param.25, bf16[512,512]{1,0:T(8,128)(2,1)} %param.35, f32[512]{0:T(512)S(1)} %bitcast.78), kind=kOutput, calls=%fused_computation.106 | convolution fusion | flops 808058112 | bytes 3412992 | tf_op jit(solution)/shard_map/dot_general | solution.py:25
  28.0 1.8 %multiply_reduce_fusion.2 = f32[768]{0:T(1024)S(1)} fusion(f32[768,512]{0,1:T(8,128)} %get-tuple-element.21, f32[768]{0:T(1024)S(1)} %broadcast_multiply_fusion.2), kind=kLoop, calls=%fused_computation.17 | loop fusion | flops 1178880 | bytes 1579008 | tf_op jit(solution)/shard_map/reduce_sum | solution.py:32
  29.9 1.3 %fusion.29 = f32[160,512]{1,0:T(8,128)S(1)} fusion(bf16[160,512]{1,0:T(8,128)(2,1)S(1)} %copy-done.5, bf16[1024,512]{1,0:T(8,128)(2,1)} %param.41), kind=kOutput, calls=%fused_computation.53 | convolution fusion | flops 83886080 | bytes 1015808 | tf_op jit(solution)/shard_map/dot_general | solution.py:25
  31.2 0.0 copy-done.2
  31.2 0.0 copy-done.3
  31.2 0.3 add_convert_fusion.2
  31.5 21.5 %all-to-all-done = bf16[16,96,512]{2,1,0:T(8,128)(2,1)S(1)} async-done(((bf16[16,96,512]{2,1,0:T(8,128)(2,1)}), bf16[16,96,512]{2,1,0:T(8,128)(2,1)S(1)}, u32[]{:S(2)}, u32[]{:S(2)}) %all-to-all-start) | async-done | bytes 1572896 | tf_op jit(solution)/shard_map/all_to_all | solution.py:99
  53.1 5.4 %gather_fusion.1 = bf16[1536,512]{1,0:T(8,128)(2,1)} fusion(bf16[1536,512]{1,0:T(8,128)(2,1)S(1)} %bitcast.61, s32[2048]{0:T(1024)S(1)} %pad_clamp_fusion.1), kind=kCustom, calls=%fused_computation.1 | custom fusion | bytes 3151872 | tf_op jit(solution)/shard_map/jit(_take)/gather | solution.py:48
  58.5 7.3 %fusion.55 = (f32[1536]{0:T(1024)S(1)}, f32[1536,512]{1,0:T(8,128)}) fusion(bf16[512,512]{1,0:T(8,128)(2,1)S(1)} %copy-done, f32[1536,512]{1,0:T(8,128)} %gather_fusion.2, bf16[1536,512]{1,0:T(8,128)(2,1)} %param.27, f32[512]{0:T(512)S(1)} %bitcast.77, bf16[1536,512]{1,0:T(8,128)(2,1)} %gather_fusion.1, pred[1536]{0:T(1024)(128)(4,1)S(1)} %get-tuple-element.30, ...), kind=kOutput, calls=%fused_computation.107 | convolution fusion | flops 1620048384 | bytes 10497024 | tf_op jit(solution)/shard_map/dot_general | solution.py:25
  65.8 2.6 %multiply_reduce_fusion = f32[1536]{0:T(1024)S(1)} fusion(f32[1536,512]{1,0:T(8,128)} %get-tuple-element.23, f32[1536]{0:T(1024)S(1)} %broadcast_multiply_fusion), kind=kLoop, calls=%fused_computation.10 | loop fusion | flops 2357760 | bytes 3158016 | tf_op jit(solution)/shard_map/reduce_sum | solution.py:32
  68.4 0.2 copy-done.1
  68.6 2.0 %add_convert_fusion = bf16[1536,512]{1,0:T(8,128)(2,1)} fusion(bf16[1536,512]{1,0:T(8,128)(2,1)S(1)} %copy-done.4, f32[1536,512]{1,0:T(8,128)S(1)} %copy-done.1, f32[512]{0:T(512)S(1)} %bitcast.72, f32[1536]{0:T(1024)S(1)} %add_rsqrt_fusion, f32[1536]{0:T(1024)S(1)} %broadcast_multiply_fusion), kind=kLoop, calls=%fused_computation.9 | loop fusion | flops 4718592 | bytes 6305792 | tf_op jit(solution)/shard_map/convert_element_type | solution.py:50
  70.6 2.2 %multiply_convert_fusion.5 = bf16[160,512]{1,0:T(8,128)(2,1)S(1)} fusion(f32[160,512]{1,0:T(8,128)S(1)} %fusion.29, bf16[1024,512]{1,0:T(8,128)(2,1)} %param.41, bf16[12,128,512]{2,1,0:T(8,128)(2,1)} %bitcast.65, s32[12,128]{1,0:T(8,128)S(1)} %bitcast.67, f32[512]{0:T(512)S(1)} %bitcast.76), kind=kOutput, calls=%fused_computation.62 | convolution fusion | flops 336445440 | bytes 2596864 | tf_op jit(solution)/shard_map/dot_general | solution.py:25
  72.8 0.4 fusion.58
  73.2 0.2 multiply_reduce_fusion.4
  73.4 0.2 add_convert_fusion.4
  73.5 1.3 %convolution_convert_fusion.1 = bf16[160,512]{1,0:T(8,128)(2,1)S(1)} fusion(bf16[160,512]{1,0:T(8,128)(2,1)S(1)} %add_convert_fusion.4, bf16[1536,512]{1,0:T(8,128)(2,1)} %param.44), kind=kOutput, calls=%fused_computation.29 | convolution fusion | flops 83968000 | bytes 851968 | tf_op jit(solution)/shard_map/dot_general | solution.py:25
  74.8 2.0 %gather_fusion.3 = bf16[512,512]{1,0:T(8,128)(2,1)S(1)} fusion(bf16[160,512]{1,0:T(8,128)(2,1)S(1)} %convolution_convert_fusion.1, s32[1024]{0:T(1024)S(1)} %pad_clamp_fusion.3), kind=kCustom, calls=%fused_computation.3 | custom fusion | bytes 1050624 | tf_op jit(solution)/shard_map/jit(_take)/gather | solution.py:65
  76.8 0.0 copy-start.19
  76.8 1.0 select_select_fusion.1
  77.8 4.7 %all-to-all-start.1 = ((bf16[16,32,512]{2,1,0:T(8,128)(2,1)}), bf16[16,32,512]{2,1,0:T(8,128)(2,1)S(1)}, u32[]{:S(2)}, u32[]{:S(2)}) async-start(bf16[16,32,512]{2,1,0:T(8,128)(2,1)} %select_select_fusion.1), calls=%async_computation.1 | async-start | bytes 1048576 | tf_op jit(solution)/shard_map/all_to_all | solution.py:127
  82.5 0.0 copy-done.19
  82.5 1.2 %copy.28 = bf16[768,512]{1,0:T(8,128)(2,1)} copy(bf16[768,512]{0,1:T(8,128)(2,1)S(1)} %add_convert_fusion.2) | data formatting | bytes 1572864
  83.7 2.1 %collective-permute-start = (bf16[40,512]{1,0:T(8,128)(2,1)S(1)}, bf16[40,512]{1,0:T(8,128)(2,1)S(1)}, u32[]{:S(2)}, u32[]{:S(2)}) collective-permute-start(bf16[40,512]{1,0:T(8,128)(2,1)S(1)} %get-tuple-element.4), channel_id=1, source_target_pairs={{0,1},{1,2},{2,3},{3,4},{4,5},{5,6},{6,7},{7,8},{8,9},{9,10},{10,1... | collective-permute-start | bytes 122888 | tf_op jit(solution)/shard_map/ppermute | solution.py:15
  85.8 4.6 %collective-permute-start.1 = (bf16[40,512]{1,0:T(8,128)(2,1)S(1)}, bf16[40,512]{1,0:T(8,128)(2,1)S(1)}, u32[]{:S(2)}, u32[]{:S(2)}) collective-permute-start(bf16[40,512]{1,0:T(8,128)(2,1)S(1)} %get-tuple-element.5), channel_id=1, source_target_pairs={{1,0},{2,1},{3,2},{4,3},{5,4},{6,5},{7,6},{8,7},{9,8},{10,9},{11,1... | collective-permute-start | bytes 122888 | tf_op jit(solution)/shard_map/ppermute | solution.py:17
  90.4 1.3 %fusion.15 = f32[160,512]{1,0:T(8,128)S(1)} fusion(bf16[160,512]{1,0:T(8,128)(2,1)S(1)} %add_convert_fusion.4, bf16[1536,512]{1,0:T(8,128)(2,1)} %param.44), kind=kOutput, calls=%fused_computation.40 | convolution fusion | flops 83886080 | bytes 1015808 | tf_op jit(solution)/shard_map/dot_general | solution.py:25
  91.7 1.3 %fusion.21 = f32[160,512]{1,0:T(8,128)S(1)} fusion(bf16[160,512]{1,0:T(8,128)(2,1)S(1)} %add_convert_fusion.4, bf16[1024,512]{1,0:T(8,128)(2,1)} %param.47), kind=kOutput, calls=%fused_computation.46 | convolution fusion | flops 83886080 | bytes 1015808 | tf_op jit(solution)/shard_map/dot_general | solution.py:25
  93.0 4.9 %gather_fusion.5 = f32[1024,512]{1,0:T(8,128)} fusion(f32[160,512]{1,0:T(8,128)S(1)} %fusion.15, s32[1024]{0:T(1024)S(1)} %fusion.40), kind=kCustom, calls=%fused_computation.5 | custom fusion | bytes 4198400 | tf_op jit(solution)/shard_map/jit(_take)/gather | solution.py:49
  97.9 0.0 collective-permute-done
  97.9 0.0 collective-permute-done.1
  97.9 0.0 all-to-all-done.1
  97.9 0.1 pad_maximum_fusion
  97.9 5.0 %gather_fusion.4 = bf16[1024,512]{1,0:T(8,128)(2,1)} fusion(bf16[752,512]{1,0:T(8,128)(2,1)S(1)} %pad_maximum_fusion, s32[1024]{0:T(1024)S(1)} %fusion.39), kind=kCustom, calls=%fused_computation.4 | custom fusion | bytes 2101248 | tf_op jit(solution)/shard_map/jit(_take)/gather | solution.py:48
  103.0 4.2 %fusion.59 = (f32[1024]{0:T(1024)S(1)}, f32[1024,512]{1,0:T(8,128)S(1)}) fusion(bf16[512,512]{1,0:T(8,128)(2,1)} %param.45, f32[1024,512]{1,0:T(8,128)} %gather_fusion.5, f32[512]{0:T(512)S(1)} %bitcast.74, bf16[1024,512]{1,0:T(8,128)(2,1)} %gather_fusion.4, pred[1024]{0:T(1024)(128)(4,1)S(1)} %get-tuple-element.32, ...), kind=kOutput, calls=%fused_computation.109 | convolution fusion | flops 1080032256 | bytes 7348224 | tf_op jit(solution)/shard_map/dot_general | solution.py:25
  107.2 0.0 copy-start.6
  107.2 0.4 multiply_reduce_fusion.1
  107.6 0.8 copy-done.6
  108.4 1.4 %add_convert_fusion.1 = bf16[1024,512]{1,0:T(8,128)(2,1)} fusion(bf16[1024,512]{1,0:T(8,128)(2,1)S(1)} %copy-done.6, f32[1024,512]{1,0:T(8,128)S(1)} %get-tuple-element.27, f32[512]{0:T(512)S(1)} %bitcast.69, f32[1024]{0:T(1024)S(1)} %add_rsqrt_fusion.1, f32[1024]{0:T(1024)S(1)} %broadcast_multiply_fusion.1), kind=kLoop, calls=%fused_computation.12 | loop fusion | flops 3145728 | bytes 4204544 | tf_op jit(solution)/shard_map/convert_element_type | solution.py:50
  109.8 2.0 %multiply_convert_fusion.4 = bf16[160,512]{1,0:T(8,128)(2,1)S(1)} fusion(f32[160,512]{1,0:T(8,128)S(1)} %fusion.21, bf16[1024,512]{1,0:T(8,128)(2,1)} %param.47, bf16[8,128,512]{2,1,0:T(8,128)(2,1)} %bitcast.66, s32[8,128]{1,0:T(8,128)S(1)} %bitcast.68, f32[512]{0:T(512)S(1)} %bitcast.75), kind=kOutput, calls=%fused_computation.58 | convolution fusion | flops 252477440 | bytes 2070528 | tf_op jit(solution)/shard_map/dot_general | solution.py:25
  111.8 0.4 fusion.62
  112.2 0.2 multiply_reduce_fusion.3
  112.4 0.8 add_convert_fusion.3
  (50 shorter events, 0.2 us)
Async XLA Ops:
  0.6 57.8 %copy-start = (bf16[512,512]{1,0:T(8,128)(2,1)S(1)}, bf16[512,512]{1,0:T(8,128)(2,1)}, u32[]{:S(2)}) copy-start(bf16[512,512]{1,0:T(8,128)(2,1)} %param.39) | copy-start | bytes 1572868
  10.3 6.3 %copy-start.7 = (bf16[768,512]{1,0:T(8,128)(2,1)S(1)}, bf16[768,512]{1,0:T(8,128)(2,1)}, u32[]{:S(2)}) copy-start(bf16[768,512]{1,0:T(8,128)(2,1)} %param.25) | copy-start | bytes 2359300
  10.3 42.7 %all-to-all-start = ((bf16[16,96,512]{2,1,0:T(8,128)(2,1)}), bf16[16,96,512]{2,1,0:T(8,128)(2,1)S(1)}, u32[]{:S(2)}, u32[]{:S(2)}) async-start(bf16[16,96,512]{2,1,0:T(8,128)(2,1)} %select_select_fusion), calls=%async_computation | async-start | bytes 3145728 | tf_op jit(solution)/shard_map/all_to_all | solution.py:99
  16.7 1.2 %copy-start.11 = (s32[1536]{0:T(1024)S(1)}, s32[1536]{0:T(1024)}, u32[]{:S(2)}) copy-start(s32[1536]{0:T(1024)} %param.30) | copy-start | bytes 18436
  16.7 1.2 %copy-start.5 = (bf16[160,512]{1,0:T(8,128)(2,1)S(1)}, bf16[160,512]{1,0:T(8,128)(2,1)}, u32[]{:S(2)}) copy-start(bf16[160,512]{1,0:T(8,128)(2,1)} %param.26) | copy-start | bytes 491524
  16.7 2.5 %copy-start.12 = (s32[1536]{0:T(1024)S(1)}, s32[1536]{0:T(1024)}, u32[]{:S(2)}) copy-start(s32[1536]{0:T(1024)} %param.31) | copy-start | bytes 18436
  16.7 2.5 %copy-start.10 = (s32[1,16,32]{2,1,0:T(8,128)S(1)}, s32[1,16,32]{2,1,0:T(8,128)}, u32[]{:S(2)}) copy-start(s32[1,16,32]{2,1,0:T(8,128)} %param.32) | copy-start | bytes 6148
  16.7 2.6 %copy-start.15 = (f32[2,512]{1,0:T(2,128)S(1)}, f32[2,512]{1,0:T(2,128)}, u32[]{:S(2)}) copy-start(f32[2,512]{1,0:T(2,128)} %param.37) | copy-start | bytes 12292
  24.3 5.5 %copy-start.16 = (f32[2,512]{1,0:T(2,128)S(1)}, f32[2,512]{1,0:T(2,128)}, u32[]{:S(2)}) copy-start(f32[2,512]{1,0:T(2,128)} %param.40) | copy-start | bytes 12292
  24.3 5.5 %copy-start.17 = (f32[2,512]{1,0:T(2,128)S(1)}, f32[2,512]{1,0:T(2,128)}, u32[]{:S(2)}) copy-start(f32[2,512]{1,0:T(2,128)} %param.43) | copy-start | bytes 12292
  24.3 5.5 %copy-start.13 = (s32[1024]{0:T(1024)S(1)}, s32[1024]{0:T(1024)}, u32[]{:S(2)}) copy-start(s32[1024]{0:T(1024)} %param.33) | copy-start | bytes 12292
  24.3 5.5 %copy-start.14 = (s32[1024]{0:T(1024)S(1)}, s32[1024]{0:T(1024)}, u32[]{:S(2)}) copy-start(s32[1024]{0:T(1024)} %param.34) | copy-start | bytes 12292
  24.3 5.6 %copy-start.18 = (f32[2,512]{1,0:T(2,128)S(1)}, f32[2,512]{1,0:T(2,128)}, u32[]{:S(2)}) copy-start(f32[2,512]{1,0:T(2,128)} %param.46) | copy-start | bytes 12292
  28.0 3.2 %copy-start.2 = (f32[768,512]{0,1:T(8,128)S(1)}, f32[768,512]{0,1:T(8,128)}, u32[]{:S(2)}) copy-start(f32[768,512]{0,1:T(8,128)} %get-tuple-element.21) | copy-start | bytes 4718596
  28.0 3.3 %copy-start.3 = (bf16[768,512]{0,1:T(8,128)(2,1)S(1)}, bf16[768,512]{0,1:T(8,128)(2,1)}, u32[]{:S(2)}) copy-start(bf16[768,512]{0,1:T(8,128)(2,1)} %copy.27) | copy-start | bytes 2359300
  58.5 9.9 %copy-start.4 = (bf16[1536,512]{1,0:T(8,128)(2,1)S(1)}, bf16[1536,512]{1,0:T(8,128)(2,1)}, u32[]{:S(2)}) copy-start(bf16[1536,512]{1,0:T(8,128)(2,1)} %param.27) | copy-start | bytes 4718596
  65.8 2.8 %copy-start.1 = (f32[1536,512]{1,0:T(8,128)S(1)}, f32[1536,512]{1,0:T(8,128)}, u32[]{:S(2)}) copy-start(f32[1536,512]{1,0:T(8,128)} %get-tuple-element.23) | copy-start | bytes 9437188
  70.5 2.2 %copy-start.8 = (bf16[512,512]{1,0:T(8,128)(2,1)S(1)}, bf16[512,512]{1,0:T(8,128)(2,1)}, u32[]{:S(2)}) copy-start(bf16[512,512]{1,0:T(8,128)(2,1)} %param.42) | copy-start | bytes 1572868
  76.8 5.7 %copy-start.19 = (f32[2,512]{1,0:T(2,128)S(1)}, f32[2,512]{1,0:T(2,128)}, u32[]{:S(2)}) copy-start(f32[2,512]{1,0:T(2,128)} %param.49) | copy-start | bytes 12292
  77.8 20.0 %all-to-all-start.1 = ((bf16[16,32,512]{2,1,0:T(8,128)(2,1)}), bf16[16,32,512]{2,1,0:T(8,128)(2,1)S(1)}, u32[]{:S(2)}, u32[]{:S(2)}) async-start(bf16[16,32,512]{2,1,0:T(8,128)(2,1)} %select_select_fusion.1), calls=%async_computation.1 | async-start | bytes 1048576 | tf_op jit(solution)/shard_map/all_to_all | solution.py:127
  83.7 14.1 %collective-permute-start = (bf16[40,512]{1,0:T(8,128)(2,1)S(1)}, bf16[40,512]{1,0:T(8,128)(2,1)S(1)}, u32[]{:S(2)}, u32[]{:S(2)}) collective-permute-start(bf16[40,512]{1,0:T(8,128)(2,1)S(1)} %get-tuple-element.4), channel_id=1, source_target_pairs={{0,1},{1,2},{2,3},{3,4},{4,5},{5,6},{6,7},{7,8},{8,9},{9,10},{10,1... | collective-permute-start | bytes 122888 | tf_op jit(solution)/shard_map/ppermute | solution.py:15
  85.8 12.1 %collective-permute-start.1 = (bf16[40,512]{1,0:T(8,128)(2,1)S(1)}, bf16[40,512]{1,0:T(8,128)(2,1)S(1)}, u32[]{:S(2)}, u32[]{:S(2)}) collective-permute-start(bf16[40,512]{1,0:T(8,128)(2,1)S(1)} %get-tuple-element.5), channel_id=1, source_target_pairs={{1,0},{2,1},{3,2},{4,3},{5,4},{6,5},{7,6},{8,7},{9,8},{10,9},{11,1... | collective-permute-start | bytes 122888 | tf_op jit(solution)/shard_map/ppermute | solution.py:17
  107.2 1.2 %copy-start.6 = (bf16[1024,512]{1,0:T(8,128)(2,1)S(1)}, bf16[1024,512]{1,0:T(8,128)(2,1)}, u32[]{:S(2)}) copy-start(bf16[1024,512]{1,0:T(8,128)(2,1)} %param.28) | copy-start | bytes 3145732
  109.8 2.0 %copy-start.9 = (bf16[512,512]{1,0:T(8,128)(2,1)S(1)}, bf16[512,512]{1,0:T(8,128)(2,1)}, u32[]{:S(2)}) copy-start(bf16[512,512]{1,0:T(8,128)(2,1)} %param.48) | copy-start | bytes 1572868
where the time goes:
time: 114 us; the launch traced here: 113 us
  local copies, waits for them, and re-layouts  30.7 us (27%)
  matrix products  28.3 us (25%)
  waiting for transfers between devices  21.5 us (19%)
  starting transfers between devices  17.6 us (15%)
  other arithmetic  14 us (12%)
    dot_general x13, matrix products, product(): return jnp.dot(left, right, preferred_element_type=jnp.float32)  28.3 us
    all_to_all x1, waiting for transfers between devices, local(): lax.all_to_all(pick_rows(own_terms, grid_slots[0]), 'band', split_axis=0,...  21.5 us
    gather x2, local copies, waits for them, and re-layouts, edge_sums(): jnp.take(sender_terms, sender_codes, axis=0).astype(jnp.float32)  10.5 us
    gather x2, local copies, waits for them, and re-layouts, edge_sums(): jnp.take(receiver_terms, jnp.minimum(receivers, mesh_count - 1), axis=0)  9.84 us
    gather x2, local copies, waits for them, and re-layouts, pick_rows(): chosen = jnp.take(table, jnp.maximum(slot_table, 0), axis=0)  6.79 us
    all_to_all x1, starting transfers between devices, local(): lax.all_to_all(pick_rows(own_terms, grid_slots[0]), 'band', split_axis=0,...  6.32 us
    reduce_sum x5, other arithmetic, mlp_tail(): spread = jnp.mean(centred * centred, axis=-1, keepdims=True)  5.15 us
    all_to_all x1, starting transfers between devices, local(): lax.all_to_all(pick_rows(own_mesh, mesh_slots[0]), 'band', split_axis=0,...  4.68 us
  transfers between devices with their start and end apart: 4, of which 1 were waited for; matrix products, arithmetic and copies ran while one was open for 21% of the time, Pallas kernels for 0%

commit v1 on v0

v1 whole, which is shorter than its diff:
```python
import functools
import typing
from typing import Any

import jax
import jax.numpy as jnp
from jax import lax
from jax.experimental import pallas as pl
from jax.experimental.pallas import tpu as pltpu
from jax.sharding import PartitionSpec as P

MESH = pl.DeviceIdType.MESH
BF = jnp.bfloat16
F32 = jnp.float32
BLOCK = 256

class Operands(typing.NamedTuple):
    grid_latent: Any
    mesh_latent: Any
    grid_edges: Any
    mesh_edges: Any
    grid_slots: Any
    grid_senders: Any
    grid_receivers: Any
    mesh_slots: Any
    mesh_senders: Any
    mesh_receivers: Any
    grid_node_in: Any
    grid_node_out: Any
    grid_node_vectors: Any
    encode_edge_in: Any
    encode_edge_out: Any
    encode_edge_vectors: Any
    encode_node_in: Any
    encode_node_out: Any
    encode_node_vectors: Any
    process_edge_in: Any
    process_edge_out: Any
    process_edge_vectors: Any
    process_node_in: Any
    process_node_out: Any
    process_node_vectors: Any


COUNT = len(Operands._fields)


def round_up(value, unit):
    return (value + unit - 1) // unit * unit


def group_size(count, rows):
    size = 1
    while size * 2 <= count and size * 2 * rows <= BLOCK:
        size *= 2
    return size


def dot(left, right):
    return jnp.dot(left, right, preferred_element_type=F32)


def branch(preact, vectors, weight_out):
    half = 0.5 * (preact + vectors[0:1, :])
    hidden = (half + half * jnp.tanh(half)).astype(BF)
    output = dot(hidden, weight_out[...])
    centred = output - jnp.mean(output, axis=-1, keepdims=True)
    spread = jnp.mean(centred * centred, axis=-1, keepdims=True)
    return centred * lax.rsqrt(spread + 1e-05) * vectors[1:2, :]


def column(row):
    n = row.shape[1]
    eye = lax.broadcasted_iota(jnp.int32, (n, n), 0) == lax.broadcasted_iota(
        jnp.int32, (n, n), 1
    )
    spread = jnp.where(eye, jnp.broadcast_to(row.astype(F32), (n, n)), 0.0)
    return jnp.sum(spread, axis=1, keepdims=True)


def onehot_rows(col, width):
    ids = lax.broadcasted_iota(jnp.int32, (1, width), 1).astype(F32)
    return jnp.where(col == ids, 1.0, 0.0).astype(BF)


def onehot_columns(row, height):
    ids = lax.broadcasted_iota(jnp.int32, (height, 1), 0).astype(F32)
    return jnp.where(ids == row.astype(F32), 1.0, 0.0).astype(BF)


def rows_at(start, size, unit=16):
    return pl.ds(pl.multiple_of(start, unit), size)


def kernel(dims, *refs):
    count, cap_g, cap_m = dims
    n_in = COUNT
    hbm = Operands(*refs[:n_in])
    grid_out, mesh_out = refs[n_in : n_in + 2]
    held = Operands(*refs[n_in + 2 : 2 * n_in + 2])
    (
        own_terms,
        send_g,
        arrived,
        sender_hot,
        receiver_hot,
        sum_hot,
        preact,
        message,
        grid_result,
        send_m,
        table,
        sender_hot_m,
        receiver_hot_m,
        sum_hot_m,
        pick_hot_m,
        preact_m,
        mesh_result,
        fetch_sem,
        out_sem,
        send_sem,
        recv_sem,
        send_sem_m,
        recv_sem_m,
        send_sem_rim,
        recv_sem_rim,
    ) = refs[2 * n_in + 2 :]
    me = lax.axis_index("band")
    width = held.grid_latent.shape[1]
    grid_rows = held.grid_latent.shape[0]
    mesh_rows = held.mesh_latent.shape[0]
    grid_edge_rows = held.grid_edges.shape[0]
    mesh_edge_rows = held.mesh_edges.shape[0]
    rim = mesh_rows // 4
    rim_held = round_up(rim, 16)
    near = mesh_rows + 2 * rim_held

    copies = Operands(
        *[
            pltpu.make_async_copy(hbm[index], held[index], fetch_sem.at[index])
            for index in range(n_in)
        ]
    )
    for copy in (
        copies.grid_slots,
        copies.grid_latent,
        copies.encode_edge_in,
        copies.grid_senders,
        copies.grid_receivers,
        copies.mesh_latent,
        copies.grid_edges,
        copies.grid_node_in,
        copies.grid_node_vectors,
        copies.grid_node_out,
        copies.mesh_slots,
        copies.mesh_senders,
        copies.mesh_receivers,
        copies.mesh_edges,
        copies.process_edge_in,
        copies.encode_node_in,
        copies.encode_edge_vectors,
        copies.encode_edge_out,
        copies.encode_node_vectors,
        copies.encode_node_out,
        copies.process_edge_vectors,
        copies.process_edge_out,
        copies.process_node_in,
        copies.process_node_vectors,
        copies.process_node_out,
    ):
        copy.start()

    barrier = pltpu.get_barrier_semaphore()

    @pl.loop(1, count)
    def _(step):
        pl.semaphore_signal(
            barrier,
            inc=1,
            device_id={"band": lax.rem(me + step, count)},
            device_id_type=MESH,
        )

    def ready(*wanted):
        for copy in wanted:
            copy.wait()

    ready(copies.grid_slots, copies.grid_latent, copies.encode_edge_in)

    @pl.loop(0, grid_rows // BLOCK)
    def _(step):
        rows = rows_at(step * BLOCK, BLOCK)
        own_terms[rows, :] = dot(
            held.grid_latent[rows, :], held.encode_edge_in[width : 2 * width, :]
        ).astype(BF)

    pl.semaphore_wait(barrier, count - 1)

    size_g = group_size(count, cap_g)
    groups_g = count // size_g
    my_group = me // size_g
    own_slot = (groups_g - 1) * size_g + lax.rem(me, size_g)

    def grid_copy(target, slot):
        return pltpu.make_async_remote_copy(
            src_ref=send_g.at[rows_at(target * cap_g, cap_g)],
            dst_ref=arrived.at[rows_at(slot * cap_g, cap_g)],
            send_sem=send_sem.at[target],
            recv_sem=recv_sem.at[slot],
            device_id={"band": target},
            device_id_type=MESH,
        )

    @pl.loop(0, groups_g)
    def _(step):
        group = lax.rem(my_group + groups_g // 2 + step, groups_g)
        hot = [
            onehot_rows(
                column(held.grid_slots[pl.ds(group * size_g + j, 1), :]), grid_rows
            )
            for j in range(size_g)
        ]
        hot = jnp.concatenate(hot, axis=0) if size_g > 1 else hot[0]
        picked = dot(hot, own_terms[...]).astype(BF)
        send_g[rows_at(group * size_g * cap_g, size_g * cap_g), :] = picked
        slot = (
            lax.rem(my_group - group - 1 + 2 * groups_g, groups_g) * size_g
            + lax.rem(me, size_g)
        )

        @pl.loop(0, size_g)
        def _(j):
            target = group * size_g + j

            @pl.when(target != me)
            def _():
                grid_copy(target, slot).start()

    arrived[rows_at(own_slot * cap_g, cap_g), :] = send_g[rows_at(me * cap_g, cap_g), :]

    ready(copies.grid_senders, copies.grid_receivers, copies.mesh_latent, copies.grid_edges)
    receiver_terms = dot(
        held.mesh_latent[...], held.encode_edge_in[2 * width :, :]
    ).astype(BF)
    base = (my_group + 1) * size_g * cap_g

    @pl.loop(0, grid_edge_rows // 128)
    def _(step):
        rows = rows_at(step * 128, 128, 128)
        codes = held.grid_senders[pl.ds(step, 1), :] - base
        codes = jnp.where(codes < 0, codes + count * cap_g, codes)
        sender_hot[rows, :] = onehot_rows(column(codes), count * cap_g)
        receivers = held.grid_receivers[pl.ds(step, 1), :]
        receiver_hot[rows, :] = onehot_rows(column(receivers), mesh_rows)
        sum_hot[:, rows] = onehot_columns(receivers, mesh_rows)

    @pl.loop(0, grid_edge_rows // BLOCK)
    def _(step):
        rows = rows_at(step * BLOCK, BLOCK)
        preact[rows, :] = dot(
            held.grid_edges[rows, :], held.encode_edge_in[:width, :]
        ) + dot(receiver_hot[rows, :], receiver_terms)

    ready(copies.grid_node_in, copies.grid_node_vectors, copies.grid_node_out)

    @pl.loop(0, grid_rows // BLOCK)
    def _(step):
        rows = rows_at(step * BLOCK, BLOCK)
        latent = held.grid_latent[rows, :]
        update = branch(
            dot(latent, held.grid_node_in[...]),
            held.grid_node_vectors,
            held.grid_node_out,
        )
        grid_result[rows, :] = (latent.astype(F32) + update).astype(BF)

    grid_store = pltpu.make_async_copy(grid_result, grid_out, out_sem.at[0])
    grid_store.start()

    ready(copies.mesh_slots, copies.mesh_senders, copies.mesh_receivers, copies.mesh_edges, copies.process_edge_in)
    near_codes = mesh_rows + 2 * rim

    @pl.loop(0, mesh_edge_rows // 128)
    def _(step):
        rows = rows_at(step * 128, 128, 128)
        codes = held.mesh_senders[pl.ds(step, 1), :]
        shift = rim_held - rim
        codes = codes + jnp.where(codes < near_codes, shift, 2 * shift)
        sender_hot_m[rows, :] = onehot_rows(column(codes), near + count * cap_m)
        receivers = held.mesh_receivers[pl.ds(step, 1), :]
        receiver_hot_m[rows, :] = onehot_rows(column(receivers), mesh_rows)
        sum_hot_m[:, rows] = onehot_columns(receivers, mesh_rows)

    @pl.loop(0, count)
    def _(step):
        slots = held.mesh_slots[pl.ds(step, 1), :]
        pick_hot_m[rows_at(step * cap_m, cap_m), :] = onehot_rows(column(slots), mesh_rows)

    @pl.loop(0, mesh_edge_rows // BLOCK)
    def _(step):
        rows = rows_at(step * BLOCK, BLOCK)
        preact_m[rows, :] = dot(
            held.mesh_edges[rows, :], held.process_edge_in[:width, :]
        )

    ready(copies.encode_node_in)
    node_preact = dot(held.mesh_latent[...], held.encode_node_in[:width, :])
    ready(copies.encode_edge_vectors, copies.encode_edge_out, copies.encode_node_vectors, copies.encode_node_out)

    part = count // 2

    def wait_for(first, last):
        @pl.loop(first, last)
        def _(slot):
            @pl.when(slot != own_slot)
            def _():
                grid_copy(lax.rem(me + 1, count), slot).wait_recv()

    wait_for(0, part)

    @pl.loop(0, grid_edge_rows // BLOCK)
    def _(step):
        rows = rows_at(step * BLOCK, BLOCK)
        preact[rows, :] += dot(sender_hot[rows, : part * cap_g], arrived[: part * cap_g, :])

    wait_for(part, count)

    @pl.loop(0, grid_edge_rows // BLOCK)
    def _(step):
        rows = rows_at(step * BLOCK, BLOCK)
        total = preact[rows, :] + dot(
            sender_hot[rows, part * cap_g :], arrived[part * cap_g :, :]
        )
        update = branch(total, held.encode_edge_vectors, held.encode_edge_out)
        message[rows, :] = (held.grid_edges[rows, :].astype(F32) + update).astype(BF)

    encode_sum = dot(sum_hot[...], message[...]).astype(BF)
    node_preact = node_preact + dot(encode_sum, held.encode_node_in[width:, :])
    middle = (
        held.mesh_latent[...].astype(F32)
        + branch(node_preact, held.encode_node_vectors, held.encode_node_out)
    ).astype(BF)

    own_mesh = dot(middle, held.process_edge_in[width : 2 * width, :]).astype(BF)
    table[rim_held : rim_held + mesh_rows, :] = own_mesh

    def far_copy(target, source):
        return pltpu.make_async_remote_copy(
            src_ref=send_m.at[rows_at(target * cap_m, cap_m)],
            dst_ref=table.at[rows_at(near + source * cap_m, cap_m)],
            send_sem=send_sem_m.at[target],
            recv_sem=recv_sem_m.at[source],
            device_id={"band": target},
            device_id_type=MESH,
        )

    size_m = group_size(count, cap_m)
    groups_m = count // size_m

    @pl.loop(0, groups_m)
    def _(step):
        group = lax.rem(me // size_m + 1 + step, groups_m)
        rows = rows_at(group * size_m * cap_m, size_m * cap_m)
        send_m[rows, :] = dot(pick_hot_m[rows, :], own_mesh).astype(BF)

        @pl.loop(0, size_m)
        def _(j):
            target = group * size_m + j

            @pl.when(target != me)
            def _():
                far_copy(target, me).start()

    to_right = pltpu.make_async_remote_copy(
        src_ref=table.at[pl.ds(rim_held + mesh_rows - rim_held, rim_held)],
        dst_ref=table.at[pl.ds(0, rim_held)],
        send_sem=send_sem_rim.at[0],
        recv_sem=recv_sem_rim.at[0],
        device_id={"band": lax.rem(me + 1, count)},
        device_id_type=MESH,
    )
    to_left = pltpu.make_async_remote_copy(
        src_ref=table.at[pl.ds(rim_held, rim_held)],
        dst_ref=table.at[pl.ds(rim_held + mesh_rows, rim_held)],
        send_sem=send_sem_rim.at[1],
        recv_sem=recv_sem_rim.at[1],
        device_id={"band": lax.rem(me + count - 1, count)},
        device_id_type=MESH,
    )
    to_right.start()
    to_left.start()
    table[rows_at(near + me * cap_m, cap_m), :] = send_m[rows_at(me * cap_m, cap_m), :]

    middle_terms = dot(middle, held.process_edge_in[2 * width :, :]).astype(BF)

    @pl.loop(0, mesh_edge_rows // BLOCK)
    def _(step):
        rows = rows_at(step * BLOCK, BLOCK)
        preact_m[rows, :] += dot(receiver_hot_m[rows, :], middle_terms)

    ready(copies.process_edge_vectors, copies.process_edge_out)
    ready(copies.process_node_in, copies.process_node_vectors, copies.process_node_out)
    node_preact = dot(middle, held.process_node_in[:width, :])

    to_right.wait_recv()
    to_left.wait_recv()

    @pl.loop(0, count)
    def _(source):
        @pl.when(source != me)
        def _():
            far_copy(lax.rem(me + 1, count), source).wait_recv()

    @pl.loop(0, mesh_edge_rows // BLOCK)
    def _(step):
        rows = rows_at(step * BLOCK, BLOCK)
        total = preact_m[rows, :] + dot(sender_hot_m[rows, :], table[...])
        update = branch(total, held.process_edge_vectors, held.process_edge_out)
        message[rows, :] = (held.mesh_edges[rows, :].astype(F32) + update).astype(BF)

    process_sum = dot(sum_hot_m[...], message[:mesh_edge_rows, :]).astype(BF)
    node_preact = node_preact + dot(process_sum, held.process_node_in[width:, :])
    mesh_result[...] = (
        middle.astype(F32)
        + branch(node_preact, held.process_node_vectors, held.process_node_out)
    ).astype(BF)
    mesh_store = pltpu.make_async_copy(mesh_result, mesh_out, out_sem.at[1])
    mesh_store.start()

    @pl.loop(0, count)
    def _(target):
        @pl.when(target != me)
        def _():
            grid_copy(target, 0).wait_send()
            far_copy(target, 0).wait_send()

    to_right.wait_send()
    to_left.wait_send()
    grid_store.wait()
    mesh_store.wait()


def pad_slots(slots, cap):
    slots = slots[0]
    if cap == slots.shape[1]:
        return slots
    return jnp.pad(slots, ((0, 0), (0, cap - slots.shape[1])), constant_values=-1)


def spread_codes(codes, slots, cap):
    return codes if cap == slots else codes // slots * cap + codes % slots


def local(*operands):
    args = Operands(*operands)
    count = lax.axis_size("band")
    slots_g = args.grid_slots.shape[2]
    slots_m = args.mesh_slots.shape[2]
    cap_g, cap_m = round_up(slots_g, 16), round_up(slots_m, 16)
    mesh_rows, width = args.mesh_latent.shape
    mesh_senders = args.mesh_senders
    if cap_m != slots_m:
        first = mesh_rows + 2 * (mesh_rows // 4)
        far = first + spread_codes(mesh_senders - first, slots_m, cap_m)
        mesh_senders = jnp.where(mesh_senders < first, mesh_senders, far)
    args = args._replace(
        grid_slots=pad_slots(args.grid_slots, cap_g),
        mesh_slots=pad_slots(args.mesh_slots, cap_m),
        grid_senders=spread_codes(args.grid_senders, slots_g, cap_g).reshape(-1, 128),
        grid_receivers=args.grid_receivers.reshape(-1, 128),
        mesh_senders=mesh_senders.reshape(-1, 128),
        mesh_receivers=args.mesh_receivers.reshape(-1, 128),
    )
    grid_rows = args.grid_latent.shape[0]
    grid_edge_rows = args.grid_edges.shape[0]
    mesh_edge_rows = args.mesh_edges.shape[0]
    near = mesh_rows + 2 * round_up(mesh_rows // 4, 16)
    edge_rows = max(grid_edge_rows, mesh_edge_rows)
    dma = pltpu.SemaphoreType.DMA
    anywhere = pl.BlockSpec(memory_space=pl.ANY)
    scratch = [pltpu.VMEM(arg.shape, arg.dtype) for arg in args]
    scratch += [
        pltpu.VMEM((grid_rows, width), BF),
        pltpu.VMEM((count * cap_g, width), BF),
        pltpu.VMEM((count * cap_g, width), BF),
        pltpu.VMEM((grid_edge_rows, count * cap_g), BF),
        pltpu.VMEM((grid_edge_rows, mesh_rows), BF),
        pltpu.VMEM((mesh_rows, grid_edge_rows), BF),
        pltpu.VMEM((grid_edge_rows, width), F32),
        pltpu.VMEM((edge_rows, width), BF),
        pltpu.VMEM((grid_rows, width), BF),
        pltpu.VMEM((count * cap_m, width), BF),
        pltpu.VMEM((near + count * cap_m, width), BF),
        pltpu.VMEM((mesh_edge_rows, near + count * cap_m), BF),
        pltpu.VMEM((mesh_edge_rows, mesh_rows), BF),
        pltpu.VMEM((mesh_rows, mesh_edge_rows), BF),
        pltpu.VMEM((count * cap_m, mesh_rows), BF),
        pltpu.VMEM((mesh_edge_rows, width), F32),
        pltpu.VMEM((mesh_rows, width), BF),
        dma((COUNT,)),
        dma((2,)),
        dma((count,)),
        dma((count,)),
        dma((count,)),
        dma((count,)),
        dma((2,)),
        dma((2,)),
    ]
    return pl.pallas_call(
        functools.partial(kernel, (count, cap_g, cap_m)),
        out_shape=(
            jax.ShapeDtypeStruct((grid_rows, width), BF),
            jax.ShapeDtypeStruct((mesh_rows, width), BF),
        ),
        in_specs=[anywhere] * COUNT,
        out_specs=(anywhere, anywhere),
        scratch_shapes=scratch,
        compiler_params=pltpu.CompilerParams(
            collective_id=0, has_side_effects=True, vmem_limit_bytes=56 * 1024 * 1024
        ),
    )(*args)


def solution(mesh):
    return jax.shard_map(
        local,
        mesh=mesh,
        in_specs=(
            P(("groups", "band"), None),
            P(("groups", "band"), None),
            P("band", None),
            P("band", None),
            P("band", None, None),
            P("band"),
            P("band"),
            P("band", None, None),
            P("band"),
            P("band"),
            P(),
            P(),
            P(),
            P(),
            P(),
            P(),
            P(),
            P(),
            P(),
            P(),
            P(),
            P(),
            P(),
            P(),
            P(),
        ),
        out_specs=(P(("groups", "band"), None), P(("groups", "band"), None)),
        check_vma=False,
    )
```

time: 114 us -> 66.7 us (0.59)
  the two profiles are of different devices: /device:TPU:16 before, /device:TPU:31 now
where the time goes in v1:
time: 66.7 us; the launch traced here: 66.5 us
  Pallas kernels  63 us (94%)
  local copies, waits for them, and re-layouts  2.77 us (4%)
    pallas_call x1, Pallas kernels, local(): pl.pallas_call(functools.partial(kernel, (count, cap_g, cap_m)), out_shap...  63 us
    unnamed x4, local copies, waits for them, and re-layouts  2.77 us

profile of v1, /device:TPU:31, one launch (start us, length us, event | category | flops | bytes accessed | tf_op | source)
XLA Modules:
  0.0 66.5 jit_solution(9718962115268041149)
XLA Ops:
  0.6 63.0 %shard_map.248 = (bf16[768,512]{1,0:T(8,128)(2,1)}, bf16[160,512]{1,0:T(8,128)(2,1)}) custom-call(bf16[768,512]{1,0:T(8,128)(2,1)} %refs_0_.1, bf16[160,512]{1,0:T(8,128)(2,1)} %refs_1_.1, bf16[1536,512]{1,0:T(8,128)(2,1)} %refs_2_.1, bf16[1024,512]{1,0:T(8,128)(2,1)} %refs_3_.1, s32[16,96]{1,0:T(8,128)} %bitcast.6, s32[12,128]{1,0:T(8,128)} %bitcast.7, ...), custom_call_target="tpu_custom_call" | custom-call | tf_op jit(solution)/shard_map/pallas_call | solution.py:509
  63.7 0.0 copy-start
  63.7 2.1 %copy.29 = bf16[768,512]{1,0:T(8,128)(2,1)} copy(bf16[768,512]{1,0:T(8,128)(2,1)} %get-tuple-element.4) | data formatting | bytes 1572864
  65.8 0.0 copy-done
  65.8 0.7 %copy.30 = bf16[160,512]{1,0:T(8,128)(2,1)} copy(bf16[160,512]{1,0:T(8,128)(2,1)S(1)} %copy-done) | data formatting | bytes 327680
Async XLA Ops:
  63.7 2.1 %copy-start = (bf16[160,512]{1,0:T(8,128)(2,1)S(1)}, bf16[160,512]{1,0:T(8,128)(2,1)}, u32[]{:S(2)}) copy-start(bf16[160,512]{1,0:T(8,128)(2,1)} %get-tuple-element.5) | copy-start | bytes 491524

commit v2 on v1

--- a/solution.py
+++ b/solution.py
@@ -199,21 +199,31 @@
     size_g = group_size(count, cap_g)
     groups_g = count // size_g
     my_group = me // size_g
-    own_slot = (groups_g - 1) * size_g + lax.rem(me, size_g)
-
-    def grid_copy(target, slot):
+    half_groups = groups_g // 2
+    quarter_groups = half_groups // 2
+    my_half, my_local = my_group // half_groups, lax.rem(my_group, half_groups)
+    my_quarter = my_local // quarter_groups
+
+    def grid_copy(target, source):
         return pltpu.make_async_remote_copy(
             src_ref=send_g.at[rows_at(target * cap_g, cap_g)],
-            dst_ref=arrived.at[rows_at(slot * cap_g, cap_g)],
+            dst_ref=arrived.at[rows_at(source * cap_g, cap_g)],
             send_sem=send_sem.at[target],
-            recv_sem=recv_sem.at[slot],
+            recv_sem=recv_sem.at[source],
             device_id={"band": target},
             device_id_type=MESH,
         )
 
     @pl.loop(0, groups_g)
     def _(step):
-        group = lax.rem(my_group + groups_g // 2 + step, groups_g)
+        half = lax.rem(my_half + 1 + step // half_groups, 2)
+        turn = lax.rem(step, half_groups)
+        quarter = lax.rem(my_quarter + turn // quarter_groups, 2)
+        group = (
+            half * half_groups
+            + quarter * quarter_groups
+            + lax.rem(my_local + turn, quarter_groups)
+        )
         hot = [
             onehot_rows(
                 column(held.grid_slots[pl.ds(group * size_g + j, 1), :]), grid_rows
@@ -223,32 +233,25 @@
         hot = jnp.concatenate(hot, axis=0) if size_g > 1 else hot[0]
         picked = dot(hot, own_terms[...]).astype(BF)
         send_g[rows_at(group * size_g * cap_g, size_g * cap_g), :] = picked
-        slot = (
-            lax.rem(my_group - group - 1 + 2 * groups_g, groups_g) * size_g
-            + lax.rem(me, size_g)
-        )
-
         @pl.loop(0, size_g)
         def _(j):
             target = group * size_g + j
 
             @pl.when(target != me)
             def _():
-                grid_copy(target, slot).start()
-
-    arrived[rows_at(own_slot * cap_g, cap_g), :] = send_g[rows_at(me * cap_g, cap_g), :]
+                grid_copy(target, me).start()
+
+    arrived[rows_at(me * cap_g, cap_g), :] = send_g[rows_at(me * cap_g, cap_g), :]
 
     ready(copies.grid_senders, copies.grid_receivers, copies.mesh_latent, copies.grid_edges)
     receiver_terms = dot(
         held.mesh_latent[...], held.encode_edge_in[2 * width :, :]
     ).astype(BF)
-    base = (my_group + 1) * size_g * cap_g
 
     @pl.loop(0, grid_edge_rows // 128)
     def _(step):
         rows = rows_at(step * 128, 128, 128)
-        codes = held.grid_senders[pl.ds(step, 1), :] - base
-        codes = jnp.where(codes < 0, codes + count * cap_g, codes)
+        codes = held.grid_senders[pl.ds(step, 1), :]
         sender_hot[rows, :] = onehot_rows(column(codes), count * cap_g)
         receivers = held.grid_receivers[pl.ds(step, 1), :]
         receiver_hot[rows, :] = onehot_rows(column(receivers), mesh_rows)
@@ -307,30 +310,39 @@
     node_preact = dot(held.mesh_latent[...], held.encode_node_in[:width, :])
     ready(copies.encode_edge_vectors, copies.encode_edge_out, copies.encode_node_vectors, copies.encode_node_out)
 
-    part = count // 2
-
-    def wait_for(first, last):
-        @pl.loop(first, last)
-        def _(slot):
-            @pl.when(slot != own_slot)
+    def wait_for(first, size):
+        @pl.loop(0, size)
+        def _(index):
+            @pl.when(first + index != me)
             def _():
-                grid_copy(lax.rem(me + 1, count), slot).wait_recv()
-
-    wait_for(0, part)
-
-    @pl.loop(0, grid_edge_rows // BLOCK)
-    def _(step):
-        rows = rows_at(step * BLOCK, BLOCK)
-        preact[rows, :] += dot(sender_hot[rows, : part * cap_g], arrived[: part * cap_g, :])
-
-    wait_for(part, count)
-
-    @pl.loop(0, grid_edge_rows // BLOCK)
-    def _(step):
-        rows = rows_at(step * BLOCK, BLOCK)
-        total = preact[rows, :] + dot(
-            sender_hot[rows, part * cap_g :], arrived[part * cap_g :, :]
-        )
+                grid_copy(lax.rem(me + 1, count), first + index).wait_recv()
+
+    def gathered(rows, first, size):
+        span = rows_at(first * cap_g, size * cap_g, 128)
+        return dot(sender_hot[rows, span], arrived[span, :])
+
+    half = count // 2
+    quarter = half // 2
+    other = (1 - my_half) * half
+    stages = (
+        (my_half * half, half),
+        (other + my_quarter * quarter, quarter),
+        (other + (1 - my_quarter) * quarter, quarter),
+    )
+    for first, size in stages[:2]:
+        wait_for(first, size)
+
+        @pl.loop(0, grid_edge_rows // BLOCK, unroll=3)
+        def _(step, first=first, size=size):
+            rows = rows_at(step * BLOCK, BLOCK)
+            preact[rows, :] += gathered(rows, first, size)
+
+    wait_for(*stages[2])
+
+    @pl.loop(0, grid_edge_rows // BLOCK, unroll=3)
+    def _(step):
+        rows = rows_at(step * BLOCK, BLOCK)
+        total = preact[rows, :] + gathered(rows, *stages[2])
         update = branch(total, held.encode_edge_vectors, held.encode_edge_out)
         message[rows, :] = (held.grid_edges[rows, :].astype(F32) + update).astype(BF)
 
@@ -359,7 +371,7 @@
 
     @pl.loop(0, groups_m)
     def _(step):
-        group = lax.rem(me // size_m + 1 + step, groups_m)
+        group = lax.rem(me // size_m + groups_m // 2 + step, groups_m)
         rows = rows_at(group * size_m * cap_m, size_m * cap_m)
         send_m[rows, :] = dot(pick_hot_m[rows, :], own_mesh).astype(BF)
 
@@ -405,16 +417,32 @@
     to_right.wait_recv()
     to_left.wait_recv()
 
-    @pl.loop(0, count)
-    def _(source):
-        @pl.when(source != me)
-        def _():
-            far_copy(lax.rem(me + 1, count), source).wait_recv()
-
-    @pl.loop(0, mesh_edge_rows // BLOCK)
-    def _(step):
-        rows = rows_at(step * BLOCK, BLOCK)
-        total = preact_m[rows, :] + dot(sender_hot_m[rows, :], table[...])
+    def wait_far(first):
+        @pl.loop(first, first + half)
+        def _(source):
+            @pl.when(source != me)
+            def _():
+                far_copy(lax.rem(me + 1, count), source).wait_recv()
+
+    def far(rows, first):
+        span = rows_at(near + first * cap_m, half * cap_m, 128)
+        return dot(sender_hot_m[rows, span], table[span, :])
+
+    wait_far(my_half * half)
+
+    @pl.loop(0, mesh_edge_rows // BLOCK, unroll=4)
+    def _(step):
+        rows = rows_at(step * BLOCK, BLOCK)
+        preact_m[rows, :] += dot(sender_hot_m[rows, :near], table[:near, :]) + far(
+            rows, my_half * half
+        )
+
+    wait_far(other)
+
+    @pl.loop(0, mesh_edge_rows // BLOCK, unroll=4)
+    def _(step):
+        rows = rows_at(step * BLOCK, BLOCK)
+        total = preact_m[rows, :] + far(rows, other)
         update = branch(total, held.process_edge_vectors, held.process_edge_out)
         message[rows, :] = (held.mesh_edges[rows, :].astype(F32) + update).astype(BF)
 

time: 66.7 us -> 63.1 us (0.946)
  the two profiles are of different devices: /device:TPU:31 before, /device:TPU:16 now
where the time goes in v2:
time: 63.1 us; the launch traced here: 62.9 us
  Pallas kernels  59.5 us (94%)
  local copies, waits for them, and re-layouts  2.77 us (4%)
  between operations  0.66 us (1%)
    pallas_call x1, Pallas kernels, local(): pl.pallas_call(functools.partial(kernel, (count, cap_g, cap_m)), out_shap...  59.5 us
    unnamed x4, local copies, waits for them, and re-layouts  2.77 us

profile of v2, /device:TPU:16, one launch (start us, length us, event | category | flops | bytes accessed | tf_op | source)
XLA Modules:
  0.0 62.9 jit_solution(9326701443417168949)
XLA Ops:
  0.6 59.5 %shard_map.248 = (bf16[768,512]{1,0:T(8,128)(2,1)}, bf16[160,512]{1,0:T(8,128)(2,1)}) custom-call(bf16[768,512]{1,0:T(8,128)(2,1)} %refs_0_.1, bf16[160,512]{1,0:T(8,128)(2,1)} %refs_1_.1, bf16[1536,512]{1,0:T(8,128)(2,1)} %refs_2_.1, bf16[1024,512]{1,0:T(8,128)(2,1)} %refs_3_.1, s32[16,96]{1,0:T(8,128)} %bitcast.6, s32[12,128]{1,0:T(8,128)} %bitcast.7, ...), custom_call_target="tpu_custom_call" | custom-call | tf_op jit(solution)/shard_map/pallas_call | solution.py:537
  60.1 0.0 copy-start
  60.1 2.1 %copy.29 = bf16[768,512]{1,0:T(8,128)(2,1)} copy(bf16[768,512]{1,0:T(8,128)(2,1)} %get-tuple-element.4) | data formatting | bytes 1572864
  62.2 0.0 copy-done
  62.2 0.7 %copy.30 = bf16[160,512]{1,0:T(8,128)(2,1)} copy(bf16[160,512]{1,0:T(8,128)(2,1)S(1)} %copy-done) | data formatting | bytes 327680
Async XLA Ops:
  60.1 2.1 %copy-start = (bf16[160,512]{1,0:T(8,128)(2,1)S(1)}, bf16[160,512]{1,0:T(8,128)(2,1)}, u32[]{:S(2)}) copy-start(bf16[160,512]{1,0:T(8,128)(2,1)} %get-tuple-element.5) | copy-start | bytes 491524

commit v3 on v2

--- a/solution.py
+++ b/solution.py
@@ -339,7 +339,7 @@
 
     wait_for(*stages[2])
 
-    @pl.loop(0, grid_edge_rows // BLOCK, unroll=3)
+    @pl.loop(0, grid_edge_rows // BLOCK, unroll=6)
     def _(step):
         rows = rows_at(step * BLOCK, BLOCK)
         total = preact[rows, :] + gathered(rows, *stages[2])

time: 63.1 us -> 62.5 us (level)
  Pallas kernels: 59.5 us -> 58.7 us
    pallas_call x1, Pallas kernels: 59.5 us -> 58.7 us  [local(): pl.pallas_call(functools.partial(kernel, (count, cap_g, cap_m)), out_shap...]
where the time goes in v3:
time: 62.5 us; the launch traced here: 62.1 us
  Pallas kernels  58.7 us (94%)
  local copies, waits for them, and re-layouts  2.77 us (4%)
  between operations  0.66 us (1%)
    pallas_call x1, Pallas kernels, local(): pl.pallas_call(functools.partial(kernel, (count, cap_g, cap_m)), out_shap...  58.7 us
    unnamed x4, local copies, waits for them, and re-layouts  2.77 us

profile of v3, /device:TPU:16, one launch (start us, length us, event | category | flops | bytes accessed | tf_op | source)
XLA Modules:
  0.0 62.1 jit_solution(12077508261059968387)
XLA Ops:
  0.6 58.7 %shard_map.248 = (bf16[768,512]{1,0:T(8,128)(2,1)}, bf16[160,512]{1,0:T(8,128)(2,1)}) custom-call(bf16[768,512]{1,0:T(8,128)(2,1)} %refs_0_.1, bf16[160,512]{1,0:T(8,128)(2,1)} %refs_1_.1, bf16[1536,512]{1,0:T(8,128)(2,1)} %refs_2_.1, bf16[1024,512]{1,0:T(8,128)(2,1)} %refs_3_.1, s32[16,96]{1,0:T(8,128)} %bitcast.6, s32[12,128]{1,0:T(8,128)} %bitcast.7, ...), custom_call_target="tpu_custom_call" | custom-call | tf_op jit(solution)/shard_map/pallas_call | solution.py:537
  59.3 0.0 copy-start
  59.3 2.1 %copy.29 = bf16[768,512]{1,0:T(8,128)(2,1)} copy(bf16[768,512]{1,0:T(8,128)(2,1)} %get-tuple-element.4) | data formatting | bytes 1572864
  61.4 0.0 copy-done
  61.4 0.7 %copy.30 = bf16[160,512]{1,0:T(8,128)(2,1)} copy(bf16[160,512]{1,0:T(8,128)(2,1)S(1)} %copy-done) | data formatting | bytes 327680
Async XLA Ops:
  59.3 2.1 %copy-start = (bf16[160,512]{1,0:T(8,128)(2,1)S(1)}, bf16[160,512]{1,0:T(8,128)(2,1)}, u32[]{:S(2)}) copy-start(bf16[160,512]{1,0:T(8,128)(2,1)} %get-tuple-element.5) | copy-start | bytes 491524
